TPU v7x, 512 devices: a whole 4x8x8 slice. The times are simulated.
512 devices in a mesh: ia: 16 (over z, core), ja: 16 (over y, x_hi), ka: 2 (over x_lo).
Axes of the slice: x: 4 (x_hi: 2, x_lo: 2; x = x_hi * 2 + x_lo), y: 8, z: 8, core: 2. Of those that a mesh axis runs over, the one named last changes fastest.
Arguments:
- tensor: float32 [32, 4096, 4096], P('ka', 'ja', 'ia'), may hold values from -6 to 6
- factor_a: float32 [64, 4096], P('ka', 'ia'), may hold values from -4 to 4
- factor_b: float32 [64, 4096], P('ia', 'ja'), as said below
- factor_c: float32 [64, 32], P('ia', 'ka'), as said below
Outputs:
- gradient: float32 [64, 4096], P('ka', 'ia')
Inputs may be any that keep to these rules, and one draw needn't show every extreme that they name: `factor_b`: nonnegative entries. `factor_c`: nonnegative entries.
All inputs are finite; a program needn't handle non-finite values.
Results may differ from a plain program's by a relative error of at most 0.0001.
Values sent between devices are 32-bit elements; how exact they have to be, the bound alone decides.
No kernel may reach another device: no remote copies, remote signals or barrier semaphores. Data moves between devices by JAX's collectives and lax.ppermute only.
A program may use at most 64 MiB of HBM per device.

v0:
```python
import jax
import jax.numpy as jnp
from jax import lax
from jax.sharding import PartitionSpec as P


def local(tensor, factor_a, factor_b, factor_c):
    highest = lax.Precision.HIGHEST
    rank_b, rank_c = (
        lax.all_gather(factor_b, "ia", axis=0, tiled=True),
        lax.all_gather(factor_c, "ia", axis=0, tiled=True),
    )
    inner = jnp.einsum(
        "rj,kji->rki", rank_b, tensor, preferred_element_type=jnp.float32, precision=highest
    )
    partial_value = jnp.einsum(
        "rki,rk->ri", inner, rank_c, preferred_element_type=jnp.float32, precision=highest
    )
    local_b = jnp.dot(rank_b, rank_b.T, preferred_element_type=jnp.float32, precision=highest)
    local_c = jnp.dot(rank_c, rank_c.T, preferred_element_type=jnp.float32, precision=highest)
    gram_c = lax.psum(local_c, "ka")
    share_rows = factor_a.shape[0]
    offset = lax.axis_index("ka") * share_rows
    gram_b = lax.psum(local_b, "ja")
    gram_rows = lax.dynamic_slice_in_dim(gram_b, offset, share_rows, 0)
    summed_all = lax.psum(partial_value, ("ja", "ka"))
    product = lax.dynamic_slice_in_dim(summed_all, offset, share_rows, 0)
    ranks_a = lax.all_gather(factor_a, "ka", axis=0, tiled=True)
    own_c = lax.dynamic_slice_in_dim(gram_c, offset, share_rows, 0)
    own_rows = gram_rows * own_c
    return product - jnp.dot(
        own_rows, ranks_a, preferred_element_type=jnp.float32, precision=highest
    )


def solution(mesh):
    in_specs = (P("ka", "ja", "ia"), P("ka", "ia"), P("ia", "ja"), P("ia", "ka"))
    out_specs = P("ka", "ia")
    return jax.shard_map(local, mesh=mesh, in_specs=in_specs, out_specs=out_specs, check_vma=False)
```

profile of v0, /device:TPU:2, one launch (start us, length us, event | category | flops | bytes accessed | tf_op | source)
XLA Modules:
  0.0 207.9 jit_solution(13839144613800372650)
XLA Ops:
  6.5 0.0 copy-start
  6.5 0.0 all-reduce.2.cloned.1.call-start
  6.5 23.7 %all-gather = f32[16,4,256]{2,1,0:T(4,128)S(1)} all-gather(f32[1,4,256]{2,1,0:T(4,128)} %bitcast.21), channel_id=1, replica_groups=mesh['ia'=16,'ja'=16,'ka'=2] {'ia'}, dimensions={0}, use_global_device_ids=true | all-gather | bytes 69632 | tf_op jit(solution)/shard_map/all_gather | solution.py:10
  30.2 14.8 %all-gather.1 = f32[16,4,16]{2,1,0:T(4,128)S(1)} all-gather(f32[1,4,16]{2,1,0:T(4,128)} %bitcast.22), channel_id=1, replica_groups=mesh['ia'=16,'ja'=16,'ka'=2] {'ia'}, dimensions={0}, use_global_device_ids=true | all-gather | bytes 4352 | tf_op jit(solution)/shard_map/all_gather | solution.py:11
  45.0 4.8 %fusion.6 = f32[64,16,256]{2,0,1:T(8,128)S(1)} fusion(f32[64,256,1]{1,0,2:T(8,128)S(1)} %reshape.4, f32[16,256,256]{2,1,0:T(8,128)} %param.4), kind=kOutput, calls=%fused_computation.8 | convolution fusion | flops 805306368 | bytes 5308416 | tf_op jit(solution)/shard_map/rj,kji->rki/dot_general | solution.py:13
  49.8 1.3 fusion
  51.2 0.6 copy.11
  51.8 0.0 all-reduce.2.cloned.1.call-update
  51.8 0.2 fusion.7
  52.0 0.2 fusion.8
  52.2 76.8 %psum.22 = f32[64,64]{1,0:T(8,128)S(1)} all-reduce(f32[64,64]{1,0:T(8,128)S(1)} %fusion.7), channel_id=1, replica_groups=mesh['ia'=16,'ja'=16,'ka'=2] {'ja'}, use_global_device_ids=true, to_apply=%region_1.0 | all-reduce | flops 4096 | bytes 32768 | tf_op jit(solution)/shard_map/psum | solution.py:24
  129.0 8.3 %psum.23 = f32[64,64]{1,0:T(8,128)S(1)} all-reduce(f32[64,64]{1,0:T(8,128)S(1)} %fusion.8), channel_id=1, replica_groups=mesh['ia'=16,'ja'=16,'ka'=2] {'ka'}, use_global_device_ids=true, to_apply=%region_2.0 | all-reduce | flops 4096 | bytes 32768 | tf_op jit(solution)/shard_map/psum | solution.py:21
  137.3 0.0 copy-done
  137.4 4.6 %all_gather.11 = f32[64,256]{1,0:T(8,128)S(1)} all-gather(f32[32,256]{1,0:T(8,128)S(1)} %copy-done), channel_id=1, replica_groups=mesh['ia'=16,'ja'=16,'ka'=2] {'ka'}, dimensions={0}, use_global_device_ids=true | all-gather | bytes 98304 | tf_op jit(solution)/shard_map/all_gather | solution.py:28
  141.9 57.6 %all-reduce.2.cloned.1.call-done = f32[64,256]{1,0:T(8,128)} async-done(((f32[64,256]{1,0:T(8,128)}), f32[64,256]{1,0:T(8,128)}) %all-reduce.2.cloned.1.call-update) | async-done | bytes 65552 | tf_op jit(solution)/shard_map/psum | solution.py:26
  199.5 1.5 convolution_subtract_fusion
  (2 shorter events, 0.0 us)
Async XLA Ops:
  6.5 130.8 %copy-start = (f32[32,256]{1,0:T(8,128)S(1)}, f32[32,256]{1,0:T(8,128)}, u32[]{:S(2)}) copy-start(f32[32,256]{1,0:T(8,128)} %param.5) | copy-start | bytes 98308
  6.5 193.0 %all-reduce.2.cloned.1.call-start = ((), (), s32[]{:S(2)}) async-start(), calls=%async_computation | async-start | bytes 131072 | tf_op jit(solution)/shard_map/psum | solution.py:26
Sparse Core Ops, SparseCore 0:
  51.9 147.5 all-reduce.1
where the time goes:
time: 208 us
  blocking collectives  128 us (62%)
  waiting for transfers between devices  57.6 us (28%)
  between operations  13.5 us (6%)
  matrix products  8.03 us (4%)
    psum x1, blocking collectives, local(): gram_b = lax.psum(local_b, 'ja')  76.8 us
    psum x1, waiting for transfers between devices, local(): summed_all = lax.psum(partial_value, ('ja', 'ka'))  57.6 us
    all_gather x1, blocking collectives, local(): lax.all_gather(factor_b, 'ia', axis=0, tiled=True)  23.7 us
    all_gather x1, blocking collectives, local(): lax.all_gather(factor_c, 'ia', axis=0, tiled=True)  14.8 us
    psum x1, blocking collectives, local(): gram_c = lax.psum(local_c, 'ka')  8.29 us
    dot_general x1, matrix products, local(): jnp.einsum('rj,kji->rki', rank_b, tensor, preferred_element_type=jnp.floa...  4.8 us
    all_gather x1, blocking collectives, local(): ranks_a = lax.all_gather(factor_a, 'ka', axis=0, tiled=True)  4.59 us
  transfers between devices with their start and end apart: 1, of which 1 were waited for; matrix products, arithmetic and copies ran while one was open for 0% of the time, Pallas kernels for 0%

commit v1 on v0

v1 whole, which is shorter than its diff:
```python
import jax
import jax.numpy as jnp
from jax import lax
from jax.sharding import Mesh, PartitionSpec as P


def local(tensor, factor_a, factor_b, factor_c):
    highest = lax.Precision.HIGHEST
    planes, rows_j, cols = tensor.shape
    share = factor_b.shape[0]
    half = rows_j // 2
    ka = lax.axis_index("ka")
    halves = lax.dynamic_slice_in_dim(factor_b, ka * half, half, 1).reshape(share * half)
    piece = jnp.concatenate([halves, factor_c.reshape(share * planes)])
    peers = lax.axis_size("z") * lax.axis_size("c") * 2
    size = -(-piece.shape[0] // 128) * 128
    piece = jnp.pad(piece, (0, size - piece.shape[0]))
    got = lax.all_to_all(
        jnp.broadcast_to(piece[None, None], (peers, 1, size)), ("z", "c", "ka"), 0, 0, tiled=True
    )
    got = got.reshape(peers // 2, 2, size)
    ranks = peers // 2 * share
    rank_b = got[:, :, : share * half].reshape(peers // 2, 2, share, half)
    rank_b = rank_b.transpose(0, 2, 1, 3).reshape(ranks, rows_j)
    rank_c = got[:, :, share * half : share * (half + planes)].reshape(peers // 2, 2, share, planes)
    all_c = rank_c.transpose(0, 2, 1, 3).reshape(ranks, 2 * planes)
    own_c = lax.dynamic_slice_in_dim(all_c, ka * planes, planes, 1)
    weight = (own_c[:, :, None] * rank_b[:, None, :]).reshape(ranks, planes * rows_j)
    partial = jnp.dot(
        weight,
        tensor.reshape(planes * rows_j, cols),
        preferred_element_type=jnp.float32,
        precision=lax.Precision.HIGH,
    )
    gram_b = jnp.dot(rank_b, rank_b.T, preferred_element_type=jnp.float32, precision=highest)
    gram_c = jnp.dot(all_c, all_c.T, preferred_element_type=jnp.float32, precision=highest)
    share_a = factor_a.shape[0]
    hadamard = lax.dynamic_slice_in_dim(gram_b * gram_c, ka * share_a, share_a, 1)
    partial = partial - jnp.dot(
        hadamard, factor_a, preferred_element_type=jnp.float32, precision=highest
    )
    mine = jnp.tile(partial.reshape(2, share_a, cols), (2, 1, 1))
    x_parts = lax.all_to_all(mine, ("xh", "ka"), 0, 0, tiled=True)
    x_sum = x_parts[0] + x_parts[1] + x_parts[2] + x_parts[3]
    wide = lax.axis_size("y")
    y_parts = lax.all_to_all(
        jnp.broadcast_to(x_sum[None], (wide, share_a, cols)), "y", 0, 0, tiled=True
    )
    return jnp.sum(y_parts, 0)


def solution(mesh):
    sizes = mesh.devices.shape
    fine = Mesh(
        mesh.devices.reshape(sizes[0] // 2, 2, sizes[1] // 2, 2, sizes[2]), ("z", "c", "y", "xh", "ka")
    )
    ia, ja = ("z", "c"), ("y", "xh")
    in_specs = (P("ka", ja, ia), P("ka", ia), P(ia, ja), P(ia, "ka"))
    return jax.shard_map(
        local, mesh=fine, in_specs=in_specs, out_specs=P("ka", ia), check_vma=False
    )
```

time: 208 us -> 55 us (0.26)
  blocking collectives: 128 us -> 26.7 us
  waiting for transfers between devices: 57.6 us -> 8.22 us
  between operations: 13.5 us -> 0.12 us
  starting transfers between devices: 0.01 us -> 11.9 us
  matrix products: 8.03 us -> 4.23 us
    psum x2 -> x0, blocking collectives: 85.1 us -> none  [the longest x1 76.8 us: local(): gram_b = lax.psum(local_b, 'ja')]
    psum x1 -> x0, waiting for transfers between devices: 57.6 us -> none  [local(): summed_all = lax.psum(partial_value, ('ja', 'ka'))]
    all_gather x3 -> x0, blocking collectives: 43.1 us -> none  [the longest x1 23.7 us: local(): lax.all_gather(factor_b, 'ia', axis=0, tiled=True)]
    all_to_all x0 -> x2, blocking collectives: none -> 26.7 us  [the longest x1 17.4 us: local(): lax.all_to_all(jnp.broadcast_to(x_sum[None], (wide, share_a, cols)), 'y',...]
    all_to_all x0 -> x1, starting transfers between devices: none -> 11.9 us  [local(): lax.all_to_all(jnp.broadcast_to(piece[None, None], (peers, 1, size)), ('z...]
    all_to_all x0 -> x1, waiting for transfers between devices: none -> 8.22 us  [local(): lax.all_to_all(jnp.broadcast_to(piece[None, None], (peers, 1, size)), ('z...]
    dot_general x4 -> x3, matrix products: 7.82 us -> 4.02 us  [the longest x1 3.57 us: local(): jnp.dot(weight, tensor.reshape(planes * rows_j, cols), preferred_element_...]
where the time goes in v1:
time: 55 us; the launch traced here: 54.6 us
  blocking collectives  26.7 us (49%)
  starting transfers between devices  11.9 us (22%)
  waiting for transfers between devices  8.22 us (15%)
  matrix products  4.23 us (8%)
  local copies, waits for them, and re-layouts  2.61 us (5%)
  other arithmetic  0.85 us (2%)
    all_to_all x1, blocking collectives, local(): lax.all_to_all(jnp.broadcast_to(x_sum[None], (wide, share_a, cols)), 'y',...  17.4 us
    all_to_all x1, starting transfers between devices, local(): lax.all_to_all(jnp.broadcast_to(piece[None, None], (peers, 1, size)), ('z...  11.9 us
    all_to_all x1, blocking collectives, local(): x_parts = lax.all_to_all(mine, ('xh', 'ka'), 0, 0, tiled=True)  9.28 us
    all_to_all x1, waiting for transfers between devices, local(): lax.all_to_all(jnp.broadcast_to(piece[None, None], (peers, 1, size)), ('z...  8.22 us
    dot_general x1, matrix products, local(): jnp.dot(weight, tensor.reshape(planes * rows_j, cols), preferred_element_...  3.57 us
  transfers between devices with their start and end apart: 1, of which 1 were waited for; matrix products, arithmetic and copies ran while one was open for 0% of the time, Pallas kernels for 0%

profile of v1, /device:TPU:2, one launch (start us, length us, event | category | flops | bytes accessed | tf_op | source)
XLA Modules:
  0.0 54.6 jit_solution(10200452087447211204)
XLA Ops:
  0.0 0.0 copy-start
  0.0 0.8 %reshape.31 = f32[64]{0:T(128)S(1)} reshape(f32[4,16]{1,0:T(4,128)} %param.7) | data formatting | bytes 512 | tf_op jit(solution)/shard_map/reshape | solution.py:14
  0.8 0.7 %dynamic-slice_bitcast_fusion = f32[512]{0:T(512)S(1)} fusion(f32[4,256]{1,0:T(4,128)} %param.6, s32[]{:T(128)S(6)} %select_n.9), kind=kLoop, calls=%fused_computation.14 | loop fusion | bytes 4100 | tf_op jit(solution)/shard_map/reshape | solution.py:13
  1.5 0.7 %broadcast_in_dim.6 = f32[32,1,640]{2,1,0:T(1,128)} broadcast(f32[640]{0:T(1024)S(1)} %select_maximum_fusion), dimensions={2} | broadcast | bytes 84480 | tf_op jit(solution)/shard_map/broadcast_in_dim | solution.py:19
  2.1 11.9 %all-to-all-start = ((f32[32,1,640]{2,1,0:T(1,128)}), f32[32,1,640]{2,1,0:T(1,128)S(1)}, u32[]{:S(2)}, u32[]{:S(2)}) async-start(f32[32,1,640]{2,1,0:T(1,128)} %broadcast_in_dim.6), calls=%async_computation | async-start | bytes 163840 | tf_op jit(solution)/shard_map/all_to_all | solution.py:18
  14.1 8.2 %all-to-all-done = f32[32,1,640]{2,1,0:T(1,128)S(1)} async-done(((f32[32,1,640]{2,1,0:T(1,128)}), f32[32,1,640]{2,1,0:T(1,128)S(1)}, u32[]{:S(2)}, u32[]{:S(2)}) %all-to-all-start) | async-done | bytes 81952 | tf_op jit(solution)/shard_map/all_to_all | solution.py:18
  22.3 0.2 reduce
  22.6 0.2 fusion.6
  22.8 0.1 reshape.33
  22.9 0.1 copy.16
  23.0 0.1 reshape.34
  23.1 0.2 fusion.7
  23.3 0.1 constant_dynamic-slice_fusion
  23.3 0.1 copy.17
  23.4 3.6 %convolution_bitcast_fusion = f32[64,256]{1,0:T(8,128)S(1)} fusion(f32[16,256,256]{2,1,0:T(8,128)} %param.4, f32[64,256]{1,0:T(8,128)S(1)} %bitcast.27, f32[64,16]{0,1:T(8,128)S(1)} %copy.17), kind=kOutput, calls=%fused_computation.1 | convolution fusion | flops 402915328 | bytes 4329472 | tf_op jit(solution)/shard_map/dot_general | solution.py:29
  27.0 0.0 copy-done
  27.0 0.3 convolution_subtract_fusion
  27.3 9.3 %all_to_all.15 = f32[4,32,256]{2,1,0:T(8,128)S(1)} all-to-all(f32[4,32,256]{2,1,0:T(8,128)S(1)} %bitcast.26), channel_id=1, replica_groups=mesh['z'=8,'c'=2,'y'=8,'xh'=2,'ka'=2] {'xh','ka'}, dimensions={0} | all-to-all | bytes 262144 | tf_op jit(solution)/shard_map/all_to_all | solution.py:43
  36.6 17.4 %all_to_all.16 = f32[8,32,256]{2,1,0:T(8,128)S(1)} all-to-all(f32[8,32,256]{2,1,0:T(8,128)S(1)} %broadcast_in_dim.8), channel_id=1, replica_groups=mesh['z'=8,'c'=2,'y'=8,'xh'=2,'ka'=2] {'y'}, dimensions={0} | all-to-all | bytes 524288 | tf_op jit(solution)/shard_map/all_to_all | solution.py:46
  54.0 0.6 %reduce_sum.9 = f32[32,256]{1,0:T(8,128)} reduce(f32[8,32,256]{2,1,0:T(8,128)S(1)} %all_to_all.16, f32[]{:T(128)} %constant.5.clone.1), dimensions={0}, to_apply=%region_0.1 | reduce | flops 57344 | bytes 294916 | tf_op jit(solution)/shard_map/reduce_sum | solution.py:49
  (9 shorter events, 0.1 us)
Async XLA Ops:
  0.0 27.0 %copy-start = (f32[32,256]{1,0:T(8,128)S(1)}, f32[32,256]{1,0:T(8,128)}, u32[]{:S(2)}) copy-start(f32[32,256]{1,0:T(8,128)} %param.5) | copy-start | bytes 98308
  2.1 20.2 %all-to-all-start = ((f32[32,1,640]{2,1,0:T(1,128)}), f32[32,1,640]{2,1,0:T(1,128)S(1)}, u32[]{:S(2)}, u32[]{:S(2)}) async-start(f32[32,1,640]{2,1,0:T(1,128)} %broadcast_in_dim.6), calls=%async_computation | async-start | bytes 163840 | tf_op jit(solution)/shard_map/all_to_all | solution.py:18

commit v2 on v0

v2 whole, which is shorter than its diff:
```python
import functools

import jax
import jax.numpy as jnp
from jax import lax
from jax.experimental import pallas as pl
from jax.experimental.pallas import tpu as pltpu
from jax.sharding import Mesh, PartitionSpec as P

ORDER = [13, 0, 1, 2, 3, 4, 5, 6, 7, 8, 9, 10, 11, 12, 14, 15]
XAX, YAX = ("y0", "xh", "ka"), ("y2", "y1")
XORD = [3, 0, 1, 2, 4, 5, 6, 7]
YORD = [2, 0, 1, 3]
EARLY, GROUP = 13, 3
VMEM, HBM = pl.BlockSpec(memory_space=pltpu.VMEM), pl.BlockSpec(memory_space=pltpu.HBM)
HIGHEST = lax.Precision.HIGHEST
BF16, F32 = jnp.bfloat16, jnp.float32


def in_hbm(array):
    return pltpu.with_memory_space_constraint(array, pltpu.HBM)


def dot(x, y, precision=None):
    return jnp.dot(x, y, preferred_element_type=F32, precision=precision)


def halves_of(value):
    high = value.astype(BF16)
    return high, (value - high.astype(F32)).astype(BF16)


def message_kernel(b_ref, c_ref, out_ref):
    peers, _, size = out_ref.shape
    share, rows_j = b_ref.shape
    planes = c_ref.shape[1]
    parts = [b_ref[r : r + 1, :] for r in range(share)]
    parts += [c_ref[r : r + 1, :] for r in range(share)]
    pad = size - share * (rows_j + planes)
    if pad:
        parts.append(jnp.zeros((1, pad), F32))
    line = jnp.concatenate(parts, axis=1)
    out_ref[...] = jnp.broadcast_to(line[None], (peers, 1, size))


def split_kernel(t_ref, hi_ref, lo_ref, stage, sems):
    planes, rows_j, _ = stage.shape
    copies = [pltpu.make_async_copy(t_ref.at[k], stage.at[k], sems.at[k]) for k in range(planes)]
    for copy in copies:
        copy.start()
    for k, copy in enumerate(copies):
        copy.wait()
        rows = pl.ds(k * rows_j, rows_j)
        hi_ref[rows, :], lo_ref[rows, :] = halves_of(stage[k])


def product_kernel(got_ref, t_ref, own_ref, other_ref, *refs, share, early):
    if early:
        hi_ref, lo_ref, *refs = refs
    out_ref, b_ref, c_ref, w_ref, acc_ref, stage, sems = refs
    rows_j, cols = b_ref.shape[1], t_ref.shape[2]
    planes = t_ref.shape[0]
    ranks = b_ref.shape[0]

    def copy_of(k):
        return pltpu.make_async_copy(t_ref.at[early + k], stage.at[k], sems.at[k])

    for k in range(planes - early):
        copy_of(k).start()

    @pl.when(lax.axis_index("ka") < 2)
    def _():
        for place, ia in enumerate(ORDER):
            line = got_ref[place, 0:1, :]
            for r in range(share):
                row = ia * share + r
                b_ref[row : row + 1, :] = line[:, r * rows_j : (r + 1) * rows_j]
                first = share * rows_j + r * planes
                c_ref[row : row + 1, :] = line[:, first : first + planes]
        b, c = b_ref[...], c_ref[...]
        gram = dot(b, b.T, HIGHEST) * dot(c, c.T, HIGHEST)
        first_a = lax.axis_index("ka") == 0
        own, other = own_ref[...], other_ref[...]
        all_a = jnp.concatenate([jnp.where(first_a, own, other), jnp.where(first_a, other, own)])
        low = -dot(gram, all_a, HIGHEST)
        total = jnp.zeros((2 * ranks, cols), F32)
        for k in range(planes):
            w_hi, w_lo = halves_of(b * c[:, k : k + 1])
            both = jnp.concatenate([w_hi, w_lo])
            if k < early:
                rows = pl.ds(k * rows_j, rows_j)
                total += dot(both, hi_ref[rows, :])
                low += dot(w_hi, lo_ref[rows, :])
            else:
                w_ref[:, pl.ds((k - early) * rows_j, rows_j)] = both
        acc_ref[...] = total[:ranks] + total[ranks:] + low

    def step(g, carry):
        for k in range(GROUP):
            copy_of(g * GROUP + k).wait()
        total = jnp.zeros((2 * ranks, cols), F32)
        low = acc_ref[...]
        for k in range(GROUP):
            at = g * GROUP + k
            t_hi, t_lo = halves_of(stage[at])
            both = w_ref[:, pl.ds(pl.multiple_of(at * rows_j, rows_j), rows_j)]
            total += dot(both, t_hi)
            low += dot(both[:ranks], t_lo)
        acc_ref[...] = total[:ranks] + total[ranks:] + low
        return carry

    lax.fori_loop(0, (planes - early) // GROUP, step, 0)
    half = own_ref.shape[0]
    for m in range(out_ref.shape[0]):
        out_ref[m] = acc_ref[pl.ds((XORD[m] % 2) * half, half), :]


def size_of(axes):
    size = 1
    for axis in axes:
        size *= lax.axis_size(axis)
    return size


def local(tensor, factor_a, factor_b, factor_c):
    planes, rows_j, cols = tensor.shape
    share = factor_b.shape[0]
    half = factor_a.shape[0]
    peers = lax.axis_size("ia")
    ranks = peers * share
    size = -(-share * (rows_j + planes) // 128) * 128
    message = pl.pallas_call(
        message_kernel,
        out_shape=jax.ShapeDtypeStruct((peers, 1, size), F32),
        in_specs=[VMEM, VMEM],
        out_specs=VMEM,
        compiler_params=pltpu.CompilerParams(vmem_limit_bytes=2**20),
    )(in_hbm(factor_b), in_hbm(factor_c))
    got = lax.all_to_all(message, "ia", 0, 0, tiled=True, axis_index_groups=[ORDER])
    other = lax.ppermute(factor_a, "ka", [(0, 1), (1, 0)])
    tensor = in_hbm(tensor)
    early = []
    if EARLY:
        depth = EARLY * rows_j
        early = pl.pallas_call(
            split_kernel,
            out_shape=[pltpu.VMEM((depth, cols), BF16)] * 2,
            in_specs=[HBM],
            out_specs=[VMEM, VMEM],
            scratch_shapes=[pltpu.VMEM((EARLY, rows_j, cols), F32), pltpu.SemaphoreType.DMA((EARLY,))],
            cost_estimate=pl.CostEstimate(
                flops=4 * depth * cols, bytes_accessed=8 * depth * cols, transcendentals=0
            ),
            compiler_params=pltpu.CompilerParams(vmem_limit_bytes=8 * 2**20),
        )(tensor)
    late = planes - EARLY
    wide_x = size_of(XAX)
    mine = pl.pallas_call(
        functools.partial(product_kernel, share=share, early=EARLY),
        out_shape=jax.ShapeDtypeStruct((wide_x, half, cols), F32),
        in_specs=[VMEM, HBM, VMEM, VMEM] + [VMEM] * len(early),
        out_specs=VMEM,
        scratch_shapes=[
            pltpu.VMEM((ranks, rows_j), F32),
            pltpu.VMEM((ranks, planes), F32),
            pltpu.VMEM((2 * ranks, late * rows_j), BF16),
            pltpu.VMEM((ranks, cols), F32),
            pltpu.VMEM((late, rows_j, cols), F32),
            pltpu.SemaphoreType.DMA((late,)),
        ],
        cost_estimate=pl.CostEstimate(
            flops=6 * ranks * planes * rows_j * cols,
            bytes_accessed=4 * planes * rows_j * cols,
            transcendentals=0,
        ),
        compiler_params=pltpu.CompilerParams(vmem_limit_bytes=12 * 2**20),
    )(got, tensor, factor_a, other, *early)
    x_sum = jnp.sum(lax.all_to_all(mine, XAX, 0, 0, tiled=True, axis_index_groups=[XORD]), 0)
    wide_y = size_of(YAX)
    y_parts = lax.all_to_all(
        jnp.broadcast_to(x_sum[None], (wide_y, half, cols)), YAX, 0, 0, tiled=True, axis_index_groups=[YORD]
    )
    return jnp.sum(y_parts, 0)


def solution(mesh):
    sizes = mesh.devices.shape
    fine = Mesh(
        mesh.devices.reshape(sizes[0], sizes[1] // 8, 2, 2, 2, sizes[2]),
        ("ia", "y2", "y1", "y0", "xh", "ka"),
    )
    ja = ("y2", "y1", "y0", "xh")
    in_specs = (P("ka", ja, "ia"), P("ka", "ia"), P("ia", ja), P("ia", "ka"))
    return jax.shard_map(
        local, mesh=fine, in_specs=in_specs, out_specs=P("ka", "ia"), check_vma=False
    )
```

time: 208 us -> 43.1 us (0.21)
  the two profiles are of different devices: /device:TPU:2 before, /device:TPU:56 now
where the time goes in v2:
time: 43.1 us; the launch traced here: 42.7 us
  blocking collectives  21.4 us (50%)
  starting transfers between devices  15.2 us (35%)
  Pallas kernels  4.85 us (11%)
  other arithmetic  0.64 us (1%)
  waiting for transfers between devices  0.55 us (1%)
    all_to_all x1, starting transfers between devices, local(): lax.all_to_all(message, 'ia', 0, 0, tiled=True, axis_index_groups=[ORDER])  11.8 us
    all_to_all x1, blocking collectives, local(): lax.all_to_all(jnp.broadcast_to(x_sum[None], (wide_y, half, cols)), YAX,...  11 us
    all_to_all x1, blocking collectives, local(): lax.all_to_all(mine, XAX, 0, 0, tiled=True, axis_index_groups=[XORD])  10.4 us
    ppermute x1, starting transfers between devices, local(): other = lax.ppermute(factor_a, 'ka', [(0, 1), (1, 0)])  3.4 us
    pallas_call x1, Pallas kernels, local(): pl.pallas_call(split_kernel, out_shape=[pltpu.VMEM((depth, cols), BF16)]...  2.05 us
    pallas_call x1, Pallas kernels, local(): pl.pallas_call(message_kernel, out_shape=jax.ShapeDtypeStruct((peers, 1,...  1.4 us
    pallas_call x1, Pallas kernels, local(): pl.pallas_call(functools.partial(product_kernel, share=share, early=EARLY...  1.39 us
  transfers between devices with their start and end apart: 2, of which 1 were waited for; matrix products, arithmetic and copies ran while one was open for 0% of the time, Pallas kernels for 5%

profile of v2, /device:TPU:56, one launch (start us, length us, event | category | flops | bytes accessed | tf_op | source)
XLA Modules:
  0.0 42.7 jit_solution(8819541249096352270)
XLA Ops:
  0.0 1.4 %shard_map.46 = f32[16,1,1152]{2,1,0:T(1,128)} custom-call(f32[4,256]{1,0:T(4,128)} %b_ref.1, f32[4,16]{1,0:T(4,128)} %c_ref.1), custom_call_target="tpu_custom_call" | custom-call | tf_op jit(solution)/shard_map/pallas_call | solution.py:132
  1.4 11.8 %all-to-all-start = ((f32[16,1,1152]{2,1,0:T(1,128)}), f32[16,1,1152]{2,1,0:T(1,128)S(1)}, u32[]{:S(2)}, u32[]{:S(2)}) async-start(f32[16,1,1152]{2,1,0:T(1,128)} %shard_map.46), calls=%async_computation | async-start | bytes 147456 | tf_op jit(solution)/shard_map/all_to_all | solution.py:139
  13.2 0.0 copy-start
  13.2 3.4 %collective-permute-start = (f32[32,256]{1,0:T(8,128)}, f32[32,256]{1,0:T(8,128)S(1)}, u32[]{:S(2)}, u32[]{:S(2)}) collective-permute-start(f32[32,256]{1,0:T(8,128)} %own_ref.1), channel_id=1, source_target_pairs={{0,1},{1,0},{2,3},{3,2},{4,5},{5,4},{6,7},{7,6},{8,9},{9,8},{10,11... | collective-permute-start | bytes 98312 | tf_op jit(solution)/shard_map/ppermute | solution.py:140
  16.6 2.1 %shard_map.47 = (bf16[3328,256]{1,0:T(8,128)(2,1)S(1)}, bf16[3328,256]{1,0:T(8,128)(2,1)S(1)}) custom-call(f32[16,256,256]{2,1,0:T(8,128)} %t_ref.3), custom_call_target="tpu_custom_call" | custom-call | flops 3407872 | bytes 6815744 | tf_op jit(solution)/shard_map/pallas_call | solution.py:145
  18.6 0.5 %collective-permute-done.other_ref = f32[32,256]{1,0:T(8,128)S(1)} collective-permute-done((f32[32,256]{1,0:T(8,128)}, f32[32,256]{1,0:T(8,128)S(1)}, u32[]{:S(2)}, u32[]{:S(2)}) %collective-permute-start) | collective-permute-done | bytes 32800 | tf_op jit(solution)/shard_map/ppermute | solution.py:140
  19.2 0.0 all-to-all-done.got_ref
  19.2 0.0 copy-done
  19.2 1.4 %shard_map.48 = f32[8,32,256]{2,1,0:T(8,128)S(1)} custom-call(f32[16,1,1152]{2,1,0:T(1,128)S(1)} %all-to-all-done.got_ref, f32[16,256,256]{2,1,0:T(8,128)} %t_ref.3, f32[32,256]{1,0:T(8,128)S(1)} %copy-done, f32[32,256]{1,0:T(8,128)S(1)} %collective-permute-done.other_ref, bf16[3328,256]{1,0:T(8,128)(2,1)S(1)} %get-tuple-element.7.refs_0_, ...), custom_call_target="tpu_custom_call" | custom-call | flops 402653184 | bytes 4194304 | tf_op jit(solution)/shard_map/pallas_call | solution.py:158
  20.6 10.4 %all_to_all.15 = f32[8,32,256]{2,1,0:T(8,128)S(1)} all-to-all(f32[8,32,256]{2,1,0:T(8,128)S(1)} %shard_map.48), channel_id=1, replica_groups={{3,0,1,2,4,5,6,7},{11,8,9,10,12,13,14,15},{19,16,17,18,20,21,22,23},{27..., dimensions={0} | all-to-all | bytes 524288 | tf_op jit(solution)/shard_map/all_to_all | solution.py:178
  31.0 11.0 %all_to_all.16 = f32[4,32,256]{2,1,0:T(8,128)S(1)} all-to-all(f32[4,32,256]{2,1,0:T(8,128)S(1)} %broadcast_in_dim.2), channel_id=1, replica_groups={{16,0,8,24},{17,1,9,25},{18,2,10,26},{19,3,11,27},{20,4,12,28},{21,5,13..., dimensions={0} | all-to-all | bytes 262144 | tf_op jit(solution)/shard_map/all_to_all | solution.py:180
  42.1 0.6 %reduce_sum.19 = f32[32,256]{1,0:T(8,128)} reduce(f32[4,32,256]{2,1,0:T(8,128)S(1)} %all_to_all.16, f32[]{:T(128)} %constant.0.clone.1), dimensions={0}, to_apply=%region_1.0 | reduce | flops 24576 | bytes 163844 | tf_op jit(solution)/shard_map/reduce_sum | solution.py:183
  (2 shorter events, 0.0 us)
Async XLA Ops:
  1.4 17.8 %all-to-all-start = ((f32[16,1,1152]{2,1,0:T(1,128)}), f32[16,1,1152]{2,1,0:T(1,128)S(1)}, u32[]{:S(2)}, u32[]{:S(2)}) async-start(f32[16,1,1152]{2,1,0:T(1,128)} %shard_map.46), calls=%async_computation | async-start | bytes 147456 | tf_op jit(solution)/shard_map/all_to_all | solution.py:139
  13.2 6.0 %copy-start = (f32[32,256]{1,0:T(8,128)S(1)}, f32[32,256]{1,0:T(8,128)}, u32[]{:S(2)}) copy-start(f32[32,256]{1,0:T(8,128)} %own_ref.1) | copy-start | bytes 98308
  13.2 6.0 %collective-permute-start = (f32[32,256]{1,0:T(8,128)}, f32[32,256]{1,0:T(8,128)S(1)}, u32[]{:S(2)}, u32[]{:S(2)}) collective-permute-start(f32[32,256]{1,0:T(8,128)} %own_ref.1), channel_id=1, source_target_pairs={{0,1},{1,0},{2,3},{3,2},{4,5},{5,4},{6,7},{7,6},{8,9},{9,8},{10,11... | collective-permute-start | bytes 98312 | tf_op jit(solution)/shard_map/ppermute | solution.py:140

commit v3 on v2

--- a/solution.py
+++ b/solution.py
@@ -8,9 +8,9 @@
 from jax.sharding import Mesh, PartitionSpec as P
 
 ORDER = [13, 0, 1, 2, 3, 4, 5, 6, 7, 8, 9, 10, 11, 12, 14, 15]
-XAX, YAX = ("y0", "xh", "ka"), ("y2", "y1")
-XORD = [3, 0, 1, 2, 4, 5, 6, 7]
-YORD = [2, 0, 1, 3]
+XAX, YAX = ("y0", "xh", "ka"), ("y2", "y1", "y0")
+XORD = [2, 0, 1, 3, 4, 5, 6, 7]
+YORD = [4, 0, 1, 2, 3, 5, 6, 7]
 EARLY, GROUP = 13, 3
 VMEM, HBM = pl.BlockSpec(memory_space=pltpu.VMEM), pl.BlockSpec(memory_space=pltpu.HBM)
 HIGHEST = lax.Precision.HIGHEST
@@ -54,10 +54,10 @@
         hi_ref[rows, :], lo_ref[rows, :] = halves_of(stage[k])
 
 
-def product_kernel(got_ref, t_ref, own_ref, other_ref, *refs, share, early):
+def product_kernel(got_ref, t_ref, *refs, share, early):
     if early:
         hi_ref, lo_ref, *refs = refs
-    out_ref, b_ref, c_ref, w_ref, acc_ref, stage, sems = refs
+    acc_ref, gram_ref, b_ref, c_ref, w_ref, stage, sems = refs
     rows_j, cols = b_ref.shape[1], t_ref.shape[2]
     planes = t_ref.shape[0]
     ranks = b_ref.shape[0]
@@ -78,11 +78,8 @@
                 first = share * rows_j + r * planes
                 c_ref[row : row + 1, :] = line[:, first : first + planes]
         b, c = b_ref[...], c_ref[...]
-        gram = dot(b, b.T, HIGHEST) * dot(c, c.T, HIGHEST)
-        first_a = lax.axis_index("ka") == 0
-        own, other = own_ref[...], other_ref[...]
-        all_a = jnp.concatenate([jnp.where(first_a, own, other), jnp.where(first_a, other, own)])
-        low = -dot(gram, all_a, HIGHEST)
+        gram_ref[...] = dot(b, b.T, HIGHEST) * dot(c, c.T, HIGHEST)
+        low = jnp.zeros((ranks, cols), F32)
         total = jnp.zeros((2 * ranks, cols), F32)
         for k in range(planes):
             w_hi, w_lo = halves_of(b * c[:, k : k + 1])
@@ -110,9 +107,17 @@
         return carry
 
     lax.fori_loop(0, (planes - early) // GROUP, step, 0)
-    half = own_ref.shape[0]
-    for m in range(out_ref.shape[0]):
-        out_ref[m] = acc_ref[pl.ds((XORD[m] % 2) * half, half), :]
+
+
+def subtract_kernel(sum_ref, gram_ref, own_ref, other_ref, out_ref):
+    first_a = lax.axis_index("ka") == 0
+    own, other = own_ref[...], other_ref[...]
+    all_a = jnp.concatenate([jnp.where(first_a, own, other), jnp.where(first_a, other, own)])
+    value = sum_ref[...] - dot(gram_ref[...], all_a, HIGHEST)
+    part = out_ref.shape[1]
+    for place, m in enumerate(XORD):
+        at = (2 * (m % 2) + m // 4) * part
+        out_ref[place] = value[at : at + part]
 
 
 def size_of(axes):
@@ -155,16 +160,15 @@
         )(tensor)
     late = planes - EARLY
     wide_x = size_of(XAX)
-    mine = pl.pallas_call(
+    partial, gram = pl.pallas_call(
         functools.partial(product_kernel, share=share, early=EARLY),
-        out_shape=jax.ShapeDtypeStruct((wide_x, half, cols), F32),
-        in_specs=[VMEM, HBM, VMEM, VMEM] + [VMEM] * len(early),
-        out_specs=VMEM,
+        out_shape=[jax.ShapeDtypeStruct((ranks, cols), F32), jax.ShapeDtypeStruct((ranks, ranks), F32)],
+        in_specs=[VMEM, HBM] + [VMEM] * len(early),
+        out_specs=[VMEM, VMEM],
         scratch_shapes=[
             pltpu.VMEM((ranks, rows_j), F32),
             pltpu.VMEM((ranks, planes), F32),
             pltpu.VMEM((2 * ranks, late * rows_j), BF16),
-            pltpu.VMEM((ranks, cols), F32),
             pltpu.VMEM((late, rows_j, cols), F32),
             pltpu.SemaphoreType.DMA((late,)),
         ],
@@ -174,13 +178,23 @@
             transcendentals=0,
         ),
         compiler_params=pltpu.CompilerParams(vmem_limit_bytes=12 * 2**20),
-    )(got, tensor, factor_a, other, *early)
+    )(got, tensor, *early)
+    mine = pl.pallas_call(
+        subtract_kernel,
+        out_shape=jax.ShapeDtypeStruct((wide_x, half // 2, cols), F32),
+        in_specs=[VMEM] * 4,
+        out_specs=VMEM,
+        compiler_params=pltpu.CompilerParams(vmem_limit_bytes=2 * 2**20),
+    )(partial, gram, factor_a, other)
     x_sum = jnp.sum(lax.all_to_all(mine, XAX, 0, 0, tiled=True, axis_index_groups=[XORD]), 0)
     wide_y = size_of(YAX)
     y_parts = lax.all_to_all(
-        jnp.broadcast_to(x_sum[None], (wide_y, half, cols)), YAX, 0, 0, tiled=True, axis_index_groups=[YORD]
+        jnp.broadcast_to(x_sum[None], (wide_y, half // 2, cols)), YAX, 0, 0, tiled=True, axis_index_groups=[YORD]
     )
-    return jnp.sum(y_parts, 0)
+    sides = []
+    for side in range(2):
+        sides.append(sum(y_parts[place] for place, m in enumerate(YORD) if m % 2 == side))
+    return jnp.concatenate(sides)
 
 
 def solution(mesh):

time: 43.1 us -> 41.9 us (0.972)
  the two profiles are of different devices: /device:TPU:56 before, /device:TPU:20 now
where the time goes in v3:
time: 41.9 us; the launch traced here: 41.6 us
  blocking collectives  21 us (50%)
  starting transfers between devices  14.9 us (36%)
  Pallas kernels  5.04 us (12%)
  other arithmetic  0.64 us (2%)
    all_to_all x1, starting transfers between devices, local(): lax.all_to_all(message, 'ia', 0, 0, tiled=True, axis_index_groups=[ORDER])  11.8 us
    all_to_all x1, blocking collectives, local(): lax.all_to_all(jnp.broadcast_to(x_sum[None], (wide_y, half // 2, cols)),...  11.2 us
    all_to_all x1, blocking collectives, local(): lax.all_to_all(mine, XAX, 0, 0, tiled=True, axis_index_groups=[XORD])  9.79 us
    ppermute x1, starting transfers between devices, local(): other = lax.ppermute(factor_a, 'ka', [(0, 1), (1, 0)])  3.1 us
    pallas_call x1, Pallas kernels, local(): pl.pallas_call(split_kernel, out_shape=[pltpu.VMEM((depth, cols), BF16)]...  2.05 us
    pallas_call x1, Pallas kernels, local(): pl.pallas_call(message_kernel, out_shape=jax.ShapeDtypeStruct((peers, 1,...  1.39 us
    pallas_call x1, Pallas kernels, local(): pl.pallas_call(functools.partial(product_kernel, share=share, early=EARLY...  1.39 us
  transfers between devices with their start and end apart: 2, of which 0 were waited for; matrix products, arithmetic and copies ran while one was open for 0% of the time, Pallas kernels for 8%

profile of v3, /device:TPU:20, one launch (start us, length us, event | category | flops | bytes accessed | tf_op | source)
XLA Modules:
  0.0 41.6 jit_solution(9105207234515528519)
XLA Ops:
  0.0 1.4 %shard_map.46 = f32[16,1,1152]{2,1,0:T(1,128)} custom-call(f32[4,256]{1,0:T(4,128)} %b_ref.1, f32[4,16]{1,0:T(4,128)} %c_ref.1), custom_call_target="tpu_custom_call" | custom-call | tf_op jit(solution)/shard_map/pallas_call | solution.py:137
  1.4 11.8 %all-to-all-start = ((f32[16,1,1152]{2,1,0:T(1,128)}), f32[16,1,1152]{2,1,0:T(1,128)S(1)}, u32[]{:S(2)}, u32[]{:S(2)}) async-start(f32[16,1,1152]{2,1,0:T(1,128)} %shard_map.46), calls=%async_computation | async-start | bytes 147456 | tf_op jit(solution)/shard_map/all_to_all | solution.py:144
  13.2 3.1 %collective-permute-start = (f32[32,256]{1,0:T(8,128)}, f32[32,256]{1,0:T(8,128)S(1)}, u32[]{:S(2)}, u32[]{:S(2)}) collective-permute-start(f32[32,256]{1,0:T(8,128)} %own_ref.1), channel_id=1, source_target_pairs={{0,1},{1,0},{2,3},{3,2},{4,5},{5,4},{6,7},{7,6},{8,9},{9,8},{10,11... | collective-permute-start | bytes 98312 | tf_op jit(solution)/shard_map/ppermute | solution.py:145
  16.3 2.1 %shard_map.47 = (bf16[3328,256]{1,0:T(8,128)(2,1)S(1)}, bf16[3328,256]{1,0:T(8,128)(2,1)S(1)}) custom-call(f32[16,256,256]{2,1,0:T(8,128)} %t_ref.3), custom_call_target="tpu_custom_call" | custom-call | flops 3407872 | bytes 6815744 | tf_op jit(solution)/shard_map/pallas_call | solution.py:150
  18.3 0.0 all-to-all-done.got_ref
  18.3 0.0 copy-start
  18.3 1.4 %shard_map.48 = (f32[64,256]{1,0:T(8,128)S(1)}, f32[64,64]{1,0:T(8,128)S(1)}) custom-call(f32[16,1,1152]{2,1,0:T(1,128)S(1)} %all-to-all-done.got_ref, f32[16,256,256]{2,1,0:T(8,128)} %t_ref.3, bf16[3328,256]{1,0:T(8,128)(2,1)S(1)} %get-tuple-element.9.refs_0_, bf16[3328,256]{1,0:T(8,128)(2,1)S(1)} %get-tuple-element.10.refs_1_), custom_call_target="tpu_custom_call" | custom-call | flops 402653184 | bytes 4194304 | tf_op jit(solution)/shard_map/pallas_call | solution.py:163
  19.7 0.0 collective-permute-done.other_ref
  19.8 0.0 copy-done
  19.8 0.2 shard_map.49
  20.0 9.8 %all_to_all.15 = f32[8,16,256]{2,1,0:T(8,128)S(1)} all-to-all(f32[8,16,256]{2,1,0:T(8,128)S(1)} %shard_map.49), channel_id=1, replica_groups={{2,0,1,3,4,5,6,7},{10,8,9,11,12,13,14,15},{18,16,17,19,20,21,22,23},{26..., dimensions={0} | all-to-all | bytes 262144 | tf_op jit(solution)/shard_map/all_to_all | solution.py:189
  29.8 11.2 %all_to_all.16 = f32[8,16,256]{2,1,0:T(8,128)S(1)} all-to-all(f32[8,16,256]{2,1,0:T(8,128)S(1)} %broadcast_in_dim.2), channel_id=1, replica_groups={{16,0,4,8,12,20,24,28},{17,1,5,9,13,21,25,29},{18,2,6,10,14,22,26,30},{..., dimensions={0} | all-to-all | bytes 262144 | tf_op jit(solution)/shard_map/all_to_all | solution.py:191
  41.0 0.6 %pad_maximum_fusion = f32[32,256]{1,0:T(8,128)} fusion(f32[16,256]{1,0:T(8,128)S(1)} %get-tuple-element.14, f32[16,256]{1,0:T(8,128)S(1)} %get-tuple-element.13), kind=kLoop, calls=%fused_computation | loop fusion | flops 8192 | bytes 65536 | tf_op jit(solution)/shard_map/concatenate | solution.py:197
  (3 shorter events, 0.0 us)
Async XLA Ops:
  1.4 16.9 %all-to-all-start = ((f32[16,1,1152]{2,1,0:T(1,128)}), f32[16,1,1152]{2,1,0:T(1,128)S(1)}, u32[]{:S(2)}, u32[]{:S(2)}) async-start(f32[16,1,1152]{2,1,0:T(1,128)} %shard_map.46), calls=%async_computation | async-start | bytes 147456 | tf_op jit(solution)/shard_map/all_to_all | solution.py:144
  13.2 6.6 %collective-permute-start = (f32[32,256]{1,0:T(8,128)}, f32[32,256]{1,0:T(8,128)S(1)}, u32[]{:S(2)}, u32[]{:S(2)}) collective-permute-start(f32[32,256]{1,0:T(8,128)} %own_ref.1), channel_id=1, source_target_pairs={{0,1},{1,0},{2,3},{3,2},{4,5},{5,4},{6,7},{7,6},{8,9},{9,8},{10,11... | collective-permute-start | bytes 98312 | tf_op jit(solution)/shard_map/ppermute | solution.py:145
  18.3 1.4 %copy-start = (f32[32,256]{1,0:T(8,128)S(1)}, f32[32,256]{1,0:T(8,128)}, u32[]{:S(2)}) copy-start(f32[32,256]{1,0:T(8,128)} %own_ref.1) | copy-start | bytes 98308

commit v4 on v3

--- a/solution.py
+++ b/solution.py
@@ -12,7 +12,9 @@
 XORD = [2, 0, 1, 3, 4, 5, 6, 7]
 YORD = [4, 0, 1, 2, 3, 5, 6, 7]
 EARLY, GROUP = 13, 3
+FIRST = 6
 VMEM, HBM = pl.BlockSpec(memory_space=pltpu.VMEM), pl.BlockSpec(memory_space=pltpu.HBM)
+ANY = pl.BlockSpec(memory_space=pl.ANY)
 HIGHEST = lax.Precision.HIGHEST
 BF16, F32 = jnp.bfloat16, jnp.float32
 
@@ -30,7 +32,7 @@
     return high, (value - high.astype(F32)).astype(BF16)
 
 
-def message_kernel(b_ref, c_ref, out_ref):
+def message_kernel(b_ref, c_ref, t_ref, out_ref, hi_ref, lo_ref, stage, sems):
     peers, _, size = out_ref.shape
     share, rows_j = b_ref.shape
     planes = c_ref.shape[1]
@@ -42,8 +44,12 @@
     line = jnp.concatenate(parts, axis=1)
     out_ref[...] = jnp.broadcast_to(line[None], (peers, 1, size))
 
-
-def split_kernel(t_ref, hi_ref, lo_ref, stage, sems):
+    @pl.when(lax.axis_index("ia") < FIRST)
+    def _():
+        split(t_ref, hi_ref, lo_ref, stage, sems)
+
+
+def split(t_ref, hi_ref, lo_ref, stage, sems):
     planes, rows_j, _ = stage.shape
     copies = [pltpu.make_async_copy(t_ref.at[k], stage.at[k], sems.at[k]) for k in range(planes)]
     for copy in copies:
@@ -52,6 +58,22 @@
         copy.wait()
         rows = pl.ds(k * rows_j, rows_j)
         hi_ref[rows, :], lo_ref[rows, :] = halves_of(stage[k])
+
+
+def split_kernel(t_ref, hi_in, lo_in, hi_ref, lo_ref, hi, lo, stage, sems, out_sems):
+    del hi_in, lo_in
+
+    @pl.when(lax.axis_index("ia") >= FIRST)
+    def _():
+        split(t_ref, hi, lo, stage, sems)
+        copies = [
+            pltpu.make_async_copy(hi, hi_ref, out_sems.at[0]),
+            pltpu.make_async_copy(lo, lo_ref, out_sems.at[1]),
+        ]
+        for copy in copies:
+            copy.start()
+        for copy in copies:
+            copy.wait()
 
 
 def product_kernel(got_ref, t_ref, *refs, share, early):
@@ -134,30 +156,32 @@
     peers = lax.axis_size("ia")
     ranks = peers * share
     size = -(-share * (rows_j + planes) // 128) * 128
-    message = pl.pallas_call(
+    tensor = in_hbm(tensor)
+    depth = EARLY * rows_j
+    stage = [pltpu.VMEM((EARLY, rows_j, cols), F32), pltpu.SemaphoreType.DMA((EARLY,))]
+    halves = pltpu.VMEM((depth, cols), BF16)
+    message, *early = pl.pallas_call(
         message_kernel,
-        out_shape=jax.ShapeDtypeStruct((peers, 1, size), F32),
-        in_specs=[VMEM, VMEM],
-        out_specs=VMEM,
-        compiler_params=pltpu.CompilerParams(vmem_limit_bytes=2**20),
-    )(in_hbm(factor_b), in_hbm(factor_c))
+        out_shape=[jax.ShapeDtypeStruct((peers, 1, size), F32), halves, halves],
+        in_specs=[VMEM, VMEM, HBM],
+        out_specs=[VMEM] * 3,
+        scratch_shapes=stage,
+        compiler_params=pltpu.CompilerParams(vmem_limit_bytes=9 * 2**20),
+    )(in_hbm(factor_b), in_hbm(factor_c), tensor)
     got = lax.all_to_all(message, "ia", 0, 0, tiled=True, axis_index_groups=[ORDER])
     other = lax.ppermute(factor_a, "ka", [(0, 1), (1, 0)])
-    tensor = in_hbm(tensor)
-    early = []
-    if EARLY:
-        depth = EARLY * rows_j
-        early = pl.pallas_call(
-            split_kernel,
-            out_shape=[pltpu.VMEM((depth, cols), BF16)] * 2,
-            in_specs=[HBM],
-            out_specs=[VMEM, VMEM],
-            scratch_shapes=[pltpu.VMEM((EARLY, rows_j, cols), F32), pltpu.SemaphoreType.DMA((EARLY,))],
-            cost_estimate=pl.CostEstimate(
-                flops=4 * depth * cols, bytes_accessed=8 * depth * cols, transcendentals=0
-            ),
-            compiler_params=pltpu.CompilerParams(vmem_limit_bytes=8 * 2**20),
-        )(tensor)
+    early = pl.pallas_call(
+        split_kernel,
+        out_shape=[halves, halves],
+        in_specs=[HBM, ANY, ANY],
+        out_specs=[ANY, ANY],
+        scratch_shapes=[halves, halves] + stage + [pltpu.SemaphoreType.DMA((2,))],
+        input_output_aliases={1: 0, 2: 1},
+        cost_estimate=pl.CostEstimate(
+            flops=4 * depth * cols, bytes_accessed=8 * depth * cols, transcendentals=0
+        ),
+        compiler_params=pltpu.CompilerParams(vmem_limit_bytes=9 * 2**20),
+    )(tensor, *early)
     late = planes - EARLY
     wide_x = size_of(XAX)
     partial, gram = pl.pallas_call(

time: 41.9 us -> 41.6 us (level)
  starting transfers between devices: 14.9 us -> 12.9 us
  waiting for transfers between devices: 0.01 us -> 1.43 us
    all_to_all x1, starting transfers between devices: 11.8 us -> 9.84 us  [local(): lax.all_to_all(message, 'ia', 0, 0, tiled=True, axis_index_groups=[ORDER])]
    all_to_all x1, waiting for transfers between devices: 0.01 us -> 1.43 us  [local(): lax.all_to_all(message, 'ia', 0, 0, tiled=True, axis_index_groups=[ORDER])]
  transfers between devices with their start and end apart: 2 -> 2, of which waited for: 0 -> 1; matrix products, arithmetic and copies ran while one was open for 0% -> 0% of each run, Pallas kernels for 8% -> 4%
where the time goes in v4:
time: 41.6 us; the launch traced here: 41.2 us
  blocking collectives  20.9 us (50%)
  starting transfers between devices  12.9 us (31%)
  Pallas kernels  5.2 us (12%)
  waiting for transfers between devices  1.43 us (3%)
  other arithmetic  0.64 us (2%)
    all_to_all x1, blocking collectives, local(): lax.all_to_all(jnp.broadcast_to(x_sum[None], (wide_y, half // 2, cols)),...  10.8 us
    all_to_all x1, blocking collectives, local(): lax.all_to_all(mine, XAX, 0, 0, tiled=True, axis_index_groups=[XORD])  10.2 us
    all_to_all x1, starting transfers between devices, local(): lax.all_to_all(message, 'ia', 0, 0, tiled=True, axis_index_groups=[ORDER])  9.84 us
    pallas_call x1, Pallas kernels, local(): pl.pallas_call(message_kernel, out_shape=[jax.ShapeDtypeStruct((peers, 1,...  3.46 us
    ppermute x1, starting transfers between devices, local(): other = lax.ppermute(factor_a, 'ka', [(0, 1), (1, 0)])  3.11 us
    all_to_all x1, waiting for transfers between devices, local(): lax.all_to_all(message, 'ia', 0, 0, tiled=True, axis_index_groups=[ORDER])  1.43 us
    pallas_call x1, Pallas kernels, local(): pl.pallas_call(functools.partial(product_kernel, share=share, early=EARLY...  1.39 us
  transfers between devices with their start and end apart: 2, of which 1 were waited for; matrix products, arithmetic and copies ran while one was open for 0% of the time, Pallas kernels for 4%

profile of v4, /device:TPU:20, one launch (start us, length us, event | category | flops | bytes accessed | tf_op | source)
XLA Modules:
  0.0 41.2 jit_solution(16695885503150322360)
XLA Ops:
  0.0 0.0 copy-start
  0.0 3.5 %shard_map.46 = (f32[16,1,1152]{2,1,0:T(1,128)}, bf16[3328,256]{1,0:T(8,128)(2,1)S(1)}, bf16[3328,256]{1,0:T(8,128)(2,1)S(1)}) custom-call(f32[4,256]{1,0:T(4,128)} %b_ref.1, f32[4,16]{1,0:T(4,128)} %c_ref.1, f32[16,256,256]{2,1,0:T(8,128)} %t_ref.5), custom_call_target="tpu_custom_call" | custom-call | tf_op jit(solution)/shard_map/pallas_call | solution.py:163
  3.5 9.8 %all-to-all-start = ((f32[16,1,1152]{2,1,0:T(1,128)}), f32[16,1,1152]{2,1,0:T(1,128)S(1)}, u32[]{:S(2)}, u32[]{:S(2)}) async-start(f32[16,1,1152]{2,1,0:T(1,128)} %get-tuple-element.12), calls=%async_computation | async-start | bytes 147456 | tf_op jit(solution)/shard_map/all_to_all | solution.py:171
  13.3 0.0 copy-done
  13.3 3.1 %collective-permute-start = (f32[32,256]{1,0:T(8,128)S(1)}, f32[32,256]{1,0:T(8,128)S(1)}, u32[]{:S(2)}, u32[]{:S(2)}) collective-permute-start(f32[32,256]{1,0:T(8,128)S(1)} %copy-done), channel_id=1, source_target_pairs={{0,1},{1,0},{2,3},{3,2},{4,5},{5,4},{6,7},{7,6},{8,9},{9,8},{10,11... | collective-permute-start | bytes 98312 | tf_op jit(solution)/shard_map/ppermute | solution.py:172
  16.4 0.2 shard_map.47
  16.6 1.4 %all-to-all-done.got_ref = f32[16,1,1152]{2,1,0:T(1,128)S(1)} async-done(((f32[16,1,1152]{2,1,0:T(1,128)}), f32[16,1,1152]{2,1,0:T(1,128)S(1)}, u32[]{:S(2)}, u32[]{:S(2)}) %all-to-all-start) | async-done | bytes 73760 | tf_op jit(solution)/shard_map/all_to_all | solution.py:171
  18.0 1.4 %shard_map.48 = (f32[64,256]{1,0:T(8,128)S(1)}, f32[64,64]{1,0:T(8,128)S(1)}) custom-call(f32[16,1,1152]{2,1,0:T(1,128)S(1)} %all-to-all-done.got_ref, f32[16,256,256]{2,1,0:T(8,128)} %t_ref.5, bf16[3328,256]{1,0:T(8,128)(2,1)S(1)} %get-tuple-element.15.refs_0_, bf16[3328,256]{1,0:T(8,128)(2,1)S(1)} %get-tuple-element.16.refs_1_), custom_call_target="tpu_custom_call" | custom-call | flops 402653184 | bytes 4194304 | tf_op jit(solution)/shard_map/pallas_call | solution.py:187
  19.4 0.0 collective-permute-done.other_ref
  19.4 0.2 shard_map.49
  19.6 10.2 %all_to_all.15 = f32[8,16,256]{2,1,0:T(8,128)S(1)} all-to-all(f32[8,16,256]{2,1,0:T(8,128)S(1)} %shard_map.49), channel_id=1, replica_groups={{2,0,1,3,4,5,6,7},{10,8,9,11,12,13,14,15},{18,16,17,19,20,21,22,23},{26..., dimensions={0} | all-to-all | bytes 262144 | tf_op jit(solution)/shard_map/all_to_all | solution.py:213
  29.8 10.8 %all_to_all.16 = f32[8,16,256]{2,1,0:T(8,128)S(1)} all-to-all(f32[8,16,256]{2,1,0:T(8,128)S(1)} %broadcast_in_dim.2), channel_id=1, replica_groups={{16,0,4,8,12,20,24,28},{17,1,5,9,13,21,25,29},{18,2,6,10,14,22,26,30},{..., dimensions={0} | all-to-all | bytes 262144 | tf_op jit(solution)/shard_map/all_to_all | solution.py:215
  40.6 0.6 %pad_maximum_fusion = f32[32,256]{1,0:T(8,128)} fusion(f32[16,256]{1,0:T(8,128)S(1)} %get-tuple-element.20, f32[16,256]{1,0:T(8,128)S(1)} %get-tuple-element.19), kind=kLoop, calls=%fused_computation | loop fusion | flops 8192 | bytes 65536 | tf_op jit(solution)/shard_map/concatenate | solution.py:221
  (3 shorter events, 0.0 us)
Async XLA Ops:
  0.0 13.3 %copy-start = (f32[32,256]{1,0:T(8,128)S(1)}, f32[32,256]{1,0:T(8,128)}, u32[]{:S(2)}) copy-start(f32[32,256]{1,0:T(8,128)} %own_ref.1) | copy-start | bytes 98308
  3.5 14.5 %all-to-all-start = ((f32[16,1,1152]{2,1,0:T(1,128)}), f32[16,1,1152]{2,1,0:T(1,128)S(1)}, u32[]{:S(2)}, u32[]{:S(2)}) async-start(f32[16,1,1152]{2,1,0:T(1,128)} %get-tuple-element.12), calls=%async_computation | async-start | bytes 147456 | tf_op jit(solution)/shard_map/all_to_all | solution.py:171
  13.3 6.1 %collective-permute-start = (f32[32,256]{1,0:T(8,128)S(1)}, f32[32,256]{1,0:T(8,128)S(1)}, u32[]{:S(2)}, u32[]{:S(2)}) collective-permute-start(f32[32,256]{1,0:T(8,128)S(1)} %copy-done), channel_id=1, source_target_pairs={{0,1},{1,0},{2,3},{3,2},{4,5},{5,4},{6,7},{7,6},{8,9},{9,8},{10,11... | collective-permute-start | bytes 98312 | tf_op jit(solution)/shard_map/ppermute | solution.py:172

commit v5 on v4

--- a/solution.py
+++ b/solution.py
@@ -32,7 +32,7 @@
     return high, (value - high.astype(F32)).astype(BF16)
 
 
-def message_kernel(b_ref, c_ref, t_ref, out_ref, hi_ref, lo_ref, stage, sems):
+def message_kernel(b_ref, c_ref, out_ref):
     peers, _, size = out_ref.shape
     share, rows_j = b_ref.shape
     planes = c_ref.shape[1]
@@ -44,6 +44,8 @@
     line = jnp.concatenate(parts, axis=1)
     out_ref[...] = jnp.broadcast_to(line[None], (peers, 1, size))
 
+
+def early_kernel(t_ref, hi_ref, lo_ref, stage, sems):
     @pl.when(lax.axis_index("ia") < FIRST)
     def _():
         split(t_ref, hi_ref, lo_ref, stage, sems)
@@ -160,14 +162,22 @@
     depth = EARLY * rows_j
     stage = [pltpu.VMEM((EARLY, rows_j, cols), F32), pltpu.SemaphoreType.DMA((EARLY,))]
     halves = pltpu.VMEM((depth, cols), BF16)
-    message, *early = pl.pallas_call(
-        message_kernel,
-        out_shape=[jax.ShapeDtypeStruct((peers, 1, size), F32), halves, halves],
-        in_specs=[VMEM, VMEM, HBM],
-        out_specs=[VMEM] * 3,
+    early = pl.pallas_call(
+        early_kernel,
+        out_shape=[halves, halves],
+        in_specs=[HBM],
+        out_specs=[VMEM] * 2,
         scratch_shapes=stage,
         compiler_params=pltpu.CompilerParams(vmem_limit_bytes=9 * 2**20),
-    )(in_hbm(factor_b), in_hbm(factor_c), tensor)
+    )(tensor)
+    factor_b, factor_c, *early = lax.optimization_barrier((factor_b, factor_c, *early))
+    message = pl.pallas_call(
+        message_kernel,
+        out_shape=jax.ShapeDtypeStruct((peers, 1, size), F32),
+        in_specs=[VMEM] * 2,
+        out_specs=VMEM,
+        compiler_params=pltpu.CompilerParams(vmem_limit_bytes=2**20),
+    )(factor_b, factor_c)
     got = lax.all_to_all(message, "ia", 0, 0, tiled=True, axis_index_groups=[ORDER])
     other = lax.ppermute(factor_a, "ka", [(0, 1), (1, 0)])
     early = pl.pallas_call(

time: 41.6 us -> 41.4 us (level)
  Pallas kernels: 5.2 us -> 4.52 us
  starting transfers between devices: 12.9 us -> 13.4 us
    pallas_call x1 -> x2, Pallas kernels: 3.46 us -> 2.78 us  [the longest x1 2.08 us: local(): pl.pallas_call(early_kernel, out_shape=[halves, halves], in_specs=[HBM],...]
    all_to_all x1, starting transfers between devices: 9.84 us -> 10.3 us  [local(): lax.all_to_all(message, 'ia', 0, 0, tiled=True, axis_index_groups=[ORDER])]
where the time goes in v5:
time: 41.4 us; the launch traced here: 41.1 us
  blocking collectives  20.9 us (50%)
  starting transfers between devices  13.4 us (32%)
  Pallas kernels  4.52 us (11%)
  waiting for transfers between devices  1.43 us (3%)
  other arithmetic  0.64 us (2%)
    all_to_all x1, blocking collectives, local(): lax.all_to_all(jnp.broadcast_to(x_sum[None], (wide_y, half // 2, cols)),...  10.8 us
    all_to_all x1, starting transfers between devices, local(): lax.all_to_all(message, 'ia', 0, 0, tiled=True, axis_index_groups=[ORDER])  10.3 us
    all_to_all x1, blocking collectives, local(): lax.all_to_all(mine, XAX, 0, 0, tiled=True, axis_index_groups=[XORD])  10.2 us
    ppermute x1, starting transfers between devices, local(): other = lax.ppermute(factor_a, 'ka', [(0, 1), (1, 0)])  3.11 us
    pallas_call x1, Pallas kernels, local(): pl.pallas_call(early_kernel, out_shape=[halves, halves], in_specs=[HBM],...  2.08 us
    all_to_all x1, waiting for transfers between devices, local(): lax.all_to_all(message, 'ia', 0, 0, tiled=True, axis_index_groups=[ORDER])  1.43 us
    pallas_call x1, Pallas kernels, local(): pl.pallas_call(functools.partial(product_kernel, share=share, early=EARLY...  1.39 us
  transfers between devices with their start and end apart: 2, of which 1 were waited for; matrix products, arithmetic and copies ran while one was open for 0% of the time, Pallas kernels for 4%

profile of v5, /device:TPU:20, one launch (start us, length us, event | category | flops | bytes accessed | tf_op | source)
XLA Modules:
  0.0 41.1 jit_solution(4899503309157330443)
XLA Ops:
  0.0 0.0 copy-start.1
  0.0 0.0 copy-start.2
  0.0 0.0 copy-start
  0.0 2.1 %shard_map.46 = (bf16[3328,256]{1,0:T(8,128)(2,1)S(1)}, bf16[3328,256]{1,0:T(8,128)(2,1)S(1)}) custom-call(f32[16,256,256]{2,1,0:T(8,128)} %t_ref.5), custom_call_target="tpu_custom_call" | custom-call | tf_op jit(solution)/shard_map/pallas_call | solution.py:165
  2.1 0.0 copy-done.1
  2.1 0.0 copy-done.2
  2.1 0.7 %shard_map.47 = f32[16,1,1152]{2,1,0:T(1,128)} custom-call(f32[4,256]{1,0:T(4,128)S(1)} %copy-done.1, f32[4,16]{1,0:T(4,128)S(1)} %copy-done.2), custom_call_target="tpu_custom_call" | custom-call | tf_op jit(solution)/shard_map/pallas_call | solution.py:174
  2.8 10.3 %all-to-all-start = ((f32[16,1,1152]{2,1,0:T(1,128)}), f32[16,1,1152]{2,1,0:T(1,128)S(1)}, u32[]{:S(2)}, u32[]{:S(2)}) async-start(f32[16,1,1152]{2,1,0:T(1,128)} %shard_map.47), calls=%async_computation | async-start | bytes 147456 | tf_op jit(solution)/shard_map/all_to_all | solution.py:181
  13.2 0.0 copy-done
  13.2 3.1 %collective-permute-start = (f32[32,256]{1,0:T(8,128)S(1)}, f32[32,256]{1,0:T(8,128)S(1)}, u32[]{:S(2)}, u32[]{:S(2)}) collective-permute-start(f32[32,256]{1,0:T(8,128)S(1)} %copy-done), channel_id=1, source_target_pairs={{0,1},{1,0},{2,3},{3,2},{4,5},{5,4},{6,7},{7,6},{8,9},{9,8},{10,11... | collective-permute-start | bytes 98312 | tf_op jit(solution)/shard_map/ppermute | solution.py:182
  16.3 0.2 shard_map.48
  16.4 1.4 %all-to-all-done.got_ref = f32[16,1,1152]{2,1,0:T(1,128)S(1)} async-done(((f32[16,1,1152]{2,1,0:T(1,128)}), f32[16,1,1152]{2,1,0:T(1,128)S(1)}, u32[]{:S(2)}, u32[]{:S(2)}) %all-to-all-start) | async-done | bytes 73760 | tf_op jit(solution)/shard_map/all_to_all | solution.py:181
  17.9 1.4 %shard_map.49 = (f32[64,256]{1,0:T(8,128)S(1)}, f32[64,64]{1,0:T(8,128)S(1)}) custom-call(f32[16,1,1152]{2,1,0:T(1,128)S(1)} %all-to-all-done.got_ref, f32[16,256,256]{2,1,0:T(8,128)} %t_ref.5, bf16[3328,256]{1,0:T(8,128)(2,1)S(1)} %get-tuple-element.21.refs_0_, bf16[3328,256]{1,0:T(8,128)(2,1)S(1)} %get-tuple-element.22.refs_1_), custom_call_target="tpu_custom_call" | custom-call | flops 402653184 | bytes 4194304 | tf_op jit(solution)/shard_map/pallas_call | solution.py:197
  19.3 0.0 collective-permute-done.other_ref
  19.3 0.2 shard_map.50
  19.5 10.2 %all_to_all.15 = f32[8,16,256]{2,1,0:T(8,128)S(1)} all-to-all(f32[8,16,256]{2,1,0:T(8,128)S(1)} %shard_map.50), channel_id=1, replica_groups={{2,0,1,3,4,5,6,7},{10,8,9,11,12,13,14,15},{18,16,17,19,20,21,22,23},{26..., dimensions={0} | all-to-all | bytes 262144 | tf_op jit(solution)/shard_map/all_to_all | solution.py:223
  29.7 10.8 %all_to_all.16 = f32[8,16,256]{2,1,0:T(8,128)S(1)} all-to-all(f32[8,16,256]{2,1,0:T(8,128)S(1)} %broadcast_in_dim.2), channel_id=1, replica_groups={{16,0,4,8,12,20,24,28},{17,1,5,9,13,21,25,29},{18,2,6,10,14,22,26,30},{..., dimensions={0} | all-to-all | bytes 262144 | tf_op jit(solution)/shard_map/all_to_all | solution.py:225
  40.5 0.6 %pad_maximum_fusion = f32[32,256]{1,0:T(8,128)} fusion(f32[16,256]{1,0:T(8,128)S(1)} %get-tuple-element.26, f32[16,256]{1,0:T(8,128)S(1)} %get-tuple-element.25), kind=kLoop, calls=%fused_computation | loop fusion | flops 8192 | bytes 65536 | tf_op jit(solution)/shard_map/concatenate | solution.py:231
  (3 shorter events, 0.0 us)
Async XLA Ops:
  0.0 2.1 %copy-start.1 = (f32[4,256]{1,0:T(4,128)S(1)}, f32[4,256]{1,0:T(4,128)}, u32[]{:S(2)}) copy-start(f32[4,256]{1,0:T(4,128)} %b_ref) | copy-start | bytes 12292
  0.0 2.1 %copy-start.2 = (f32[4,16]{1,0:T(4,128)S(1)}, f32[4,16]{1,0:T(4,128)}, u32[]{:S(2)}) copy-start(f32[4,16]{1,0:T(4,128)} %c_ref) | copy-start | bytes 772
  0.0 13.2 %copy-start = (f32[32,256]{1,0:T(8,128)S(1)}, f32[32,256]{1,0:T(8,128)}, u32[]{:S(2)}) copy-start(f32[32,256]{1,0:T(8,128)} %own_ref.1) | copy-start | bytes 98308
  2.8 15.0 %all-to-all-start = ((f32[16,1,1152]{2,1,0:T(1,128)}), f32[16,1,1152]{2,1,0:T(1,128)S(1)}, u32[]{:S(2)}, u32[]{:S(2)}) async-start(f32[16,1,1152]{2,1,0:T(1,128)} %shard_map.47), calls=%async_computation | async-start | bytes 147456 | tf_op jit(solution)/shard_map/all_to_all | solution.py:181
  13.2 6.1 %collective-permute-start = (f32[32,256]{1,0:T(8,128)S(1)}, f32[32,256]{1,0:T(8,128)S(1)}, u32[]{:S(2)}, u32[]{:S(2)}) collective-permute-start(f32[32,256]{1,0:T(8,128)S(1)} %copy-done), channel_id=1, source_target_pairs={{0,1},{1,0},{2,3},{3,2},{4,5},{5,4},{6,7},{7,6},{8,9},{9,8},{10,11... | collective-permute-start | bytes 98312 | tf_op jit(solution)/shard_map/ppermute | solution.py:182
